TPU v7x, 32 devices: a whole 2x2x4 slice. The times are simulated.
32 devices in a mesh: seq: 8 (over z, x), head: 4 (over y, core).
Axes of the slice: x: 2, y: 2, z: 4, core: 2. Of those that a mesh axis runs over, the one named last changes fastest.
Arguments:
- layer_input: bfloat16 [2048, 4096], P('seq', 'head'), may hold values from -6 to 6
- value_weight: bfloat16 [4096, 4096], P(None, 'head'), may hold values from -0.09375 to 0.09375
- state_weight: bfloat16 [4096, 2048], P(None, 'head'), may hold values from -0.02734375 to 0.02734375
- output_weight: bfloat16 [4096, 4096], P('head'), may hold values from -0.09375 to 0.09375
- log_decay: float32 [64, 2048], P('head', 'seq'), may hold values from -1.5 to 0, as said below
- skip_gain: float32 [64], P('head'), may hold values from 0.5 to 1.5
- output_grad: bfloat16 [2048, 4096], P('seq', 'head'), may hold values from -6 to 6
Outputs:
- layer_output: bfloat16 [2048, 4096], P('seq', 'head')
- input_grad: bfloat16 [2048, 4096], P('seq', 'head')
Inputs may be any that keep to these rules, and one draw needn't show every extreme that they name: `log_decay`: each entry is below zero.
All inputs are finite; a program needn't handle non-finite values.
Results may differ from a plain program's by a relative error of at most 0.015.
Values may be sent and summed in bfloat16 or wider, within the bound.
A program may use at most 64 MiB of HBM per device.

v0:
```python
import jax
import jax.numpy as jnp
from jax import lax
from jax.sharding import PartitionSpec as P

STATE = 128
BLOCK = 256


highest = lax.Precision.HIGHEST


def block_step(carried, pieces):
    values, writer, reader, decays = pieces
    running = jnp.cumsum(decays, axis=-1)
    inflow = jnp.sqrt(-jnp.expm1(2.0 * decays))
    length = decays.shape[-1]
    causal = jnp.arange(length)[:, None] >= jnp.arange(length)[None, :]
    spread = running[..., :, None] - running[..., None, :]
    kernel = jnp.where(causal, jnp.exp(jnp.where(causal, spread, 0.0)), 0.0)
    scores = jnp.einsum("tgn,sgn->gts", reader, writer, precision=highest)
    weights = scores[:, None] * kernel * inflow[..., None, :]
    within = jnp.einsum("ghts,sghp->tghp", weights, values, precision=highest)
    entering = jnp.transpose(jnp.exp(running), (2, 0, 1))[..., None]
    carried_part = jnp.einsum("tgn,ghnp->tghp", reader, carried, precision=highest) * entering
    to_end = jnp.exp(running[..., -1:] - running) * inflow
    fresh_part = jnp.einsum("sgn,ghs,sghp->ghnp", writer, to_end, values, precision=highest)
    carried = jnp.exp(running[..., -1])[..., None, None] * carried + fresh_part
    return (carried, within + carried_part)


def scan_blocks(values, writer, reader, decays, carried, block_rows):
    total_rows, group_count, per_group, head_width = values.shape
    block_count = total_rows // block_rows
    pieces = (
        values.reshape(block_count, block_rows, group_count, per_group, head_width),
        writer.reshape(block_count, block_rows, group_count, writer.shape[-1]),
        reader.reshape(block_count, block_rows, group_count, reader.shape[-1]),
        jnp.moveaxis(decays.reshape(group_count, per_group, block_count, block_rows), 2, 0),
    )
    carried, outputs = lax.scan(block_step, carried, pieces)
    return (carried, outputs.reshape(total_rows, group_count, per_group, head_width))


def per_device(
    layer_input, value_weight, state_weight, output_weight, log_decay, skip_gain, output_grad
):
    local_rows = layer_input.shape[0]
    value_width = value_weight.shape[1]
    pair_width = state_weight.shape[1]
    head_count = log_decay.shape[0]
    group_count = pair_width // (2 * STATE)
    per_group = head_count // group_count
    head_width = value_width // head_count
    block_rows = min(BLOCK, local_rows)
    contract_last = (((1,), (1,)), ((), ()))
    input_piece = lax.all_gather(layer_input, "head", axis=1, tiled=True)
    grad_piece = lax.all_gather(output_grad, "head", axis=1, tiled=True)
    value_sum = jnp.dot(input_piece, value_weight, preferred_element_type=jnp.float32)
    pair_sum = jnp.dot(input_piece, state_weight, preferred_element_type=jnp.float32)
    grad_sum = lax.dot_general(
        grad_piece, output_weight, contract_last, preferred_element_type=jnp.float32
    )
    values = lax.optimization_barrier(value_sum.astype(jnp.bfloat16))
    pair_rows = lax.optimization_barrier(pair_sum.astype(jnp.bfloat16))
    mixed_grad = grad_sum.astype(jnp.bfloat16)
    value_input = values.astype(jnp.float32)
    pair_input = pair_rows.astype(jnp.float32)
    grad_input = mixed_grad.astype(jnp.float32)
    decays = log_decay.reshape(group_count, per_group, local_rows)
    skip_gains = skip_gain.reshape(group_count, per_group)

    def local_pass(value_part, pair_part):
        head_values = value_part.reshape(local_rows, group_count, per_group, head_width)
        pair_split = pair_part.reshape(local_rows, group_count, 2, STATE)
        zero_state = jnp.zeros((group_count, per_group, STATE, head_width), jnp.float32)
        final_state, outputs = scan_blocks(
            head_values, pair_split[:, :, 0], pair_split[:, :, 1], decays, zero_state, block_rows
        )
        outputs = outputs + skip_gains[None, :, :, None] * head_values
        return (outputs.reshape(local_rows, value_width), final_state)

    (local_mixed, end_state), pullback = jax.vjp(local_pass, value_input, pair_input)
    running = jnp.cumsum(decays, axis=-1)
    entering = jnp.transpose(jnp.exp(running), (2, 0, 1))[..., None]
    decay_total = running[..., -1]
    readers = pair_input.reshape(local_rows, group_count, 2, STATE)[:, :, 1]
    grad_heads = grad_input.reshape(local_rows, group_count, per_group, head_width)
    grad_state = jnp.einsum("tgn,tghp->ghnp", readers, grad_heads * entering, precision=highest)
    all_totals, all_ends, all_grads = (
        lax.all_gather(decay_total[None].astype(jnp.bfloat16), "seq", axis=0, tiled=True).astype(
            jnp.float32
        ),
        lax.all_gather(end_state[None].astype(jnp.bfloat16), "seq", axis=0, tiled=True).astype(
            jnp.float32
        ),
        lax.all_gather(grad_state[None].astype(jnp.bfloat16), "seq", axis=0, tiled=True).astype(
            jnp.float32
        ),
    )
    position = lax.axis_index("seq")
    prefix = jnp.cumsum(all_totals, axis=0)
    prefix_here = lax.dynamic_index_in_dim(prefix, position, 0, keepdims=False)
    ordinal = jnp.arange(all_totals.shape[0], dtype=jnp.int32)[:, None, None]
    earlier_mask = ordinal < position
    later_mask = ordinal > position
    forward_gap = (prefix_here - decay_total)[None] - prefix
    forward_weight = jnp.where(
        earlier_mask, jnp.exp(jnp.where(earlier_mask, forward_gap, 0.0)), 0.0
    )
    backward_gap = prefix - all_totals - prefix_here[None]
    backward_weight = jnp.where(later_mask, jnp.exp(jnp.where(later_mask, backward_gap, 0.0)), 0.0)
    incoming = jnp.einsum("sgh,sghnp->ghnp", forward_weight, all_ends, precision=highest)
    outgoing = jnp.einsum("sgh,sghnp->ghnp", backward_weight, all_grads, precision=highest)

    def carried_pass(pair_part):
        reader_part = pair_part.reshape(local_rows, group_count, 2, STATE)[:, :, 1]
        carried_out = (
            jnp.einsum("tgn,ghnp->tghp", reader_part, incoming, precision=highest) * entering
        )
        return carried_out.reshape(local_rows, value_width)

    carried_mixed, carried_pull = jax.vjp(carried_pass, pair_input)
    mixer_out = (local_mixed + carried_mixed).astype(jnp.bfloat16)
    partial_output = jnp.dot(mixer_out, output_weight, preferred_element_type=jnp.float32)
    layer_output = lax.psum_scatter(
        partial_output.astype(jnp.bfloat16), "head", scatter_dimension=1, tiled=True
    )
    value_grad, pair_grad = pullback((grad_input, outgoing))
    pair_grad = pair_grad + carried_pull(grad_input)[0]
    partial_grad = lax.dot_general(
        value_grad.astype(jnp.bfloat16),
        value_weight,
        contract_last,
        preferred_element_type=jnp.float32,
    )
    partial_grad = partial_grad + lax.dot_general(
        pair_grad.astype(jnp.bfloat16),
        state_weight,
        contract_last,
        preferred_element_type=jnp.float32,
    )
    input_grad = lax.psum_scatter(
        partial_grad.astype(jnp.bfloat16), "head", scatter_dimension=1, tiled=True
    )
    return (layer_output, input_grad)


def solution(mesh):
    in_specs = (
        P("seq", "head"),
        P(None, "head"),
        P(None, "head"),
        P("head", None),
        P("head", "seq"),
        P("head"),
        P("seq", "head"),
    )
    out_specs = (P("seq", "head"), P("seq", "head"))
    return jax.shard_map(
        per_device, mesh=mesh, in_specs=in_specs, out_specs=out_specs, check_vma=False
    )
```

profile of v0, /device:TPU:0, one launch (start us, length us, event | category | flops | bytes accessed | tf_op | source)
XLA Modules:
  0.0 235.1 jit_solution(10357368474243667172)
XLA Ops:
  7.2 0.0 all-gather.7.cloned.1.call-start
  7.2 0.7 all-gather.7.cloned.1.call-update
  7.9 0.0 all-gather.9.cloned.1.call-start
  7.9 0.7 all-gather.9.cloned.1.call-update
  8.6 0.0 all-gather.11.cloned.1.call-start
  8.7 2.2 reduce-window.18
  10.9 0.2 slice_reduce_fusion
  11.1 0.1 exponential_bitcast_fusion
  11.2 0.2 slice_reduce_fusion.1
  11.4 0.8 multiply_bitcast_fusion
  12.2 22.7 %all-gather.7.cloned.1.call-done = bf16[256,4096]{1,0:T(8,128)(2,1)} async-done(((bf16[256,1024]{1,0:T(8,128)(2,1)}), bf16[256,4096]{1,0:T(8,128)(2,1)}) %all-gather.7.cloned.1.call-update) | async-done | bytes 2097168 | tf_op jit(solution)/shard_map/all_gather | solution.py:57
  34.9 6.5 %convolution_convert_fusion.2 = bf16[256,1024]{1,0:T(8,128)(2,1)S(1)} fusion(bf16[256,4096]{1,0:T(8,128)(2,1)} %all-gather.7.cloned.1.call-done, bf16[4096,1024]{1,0:T(8,128)(2,1)} %param.8), kind=kOutput, calls=%fused_computation.33 | convolution fusion | flops 2147745792 | bytes 11010048 | tf_op jit(solution)/shard_map/dot_general | solution.py:59
  41.4 0.0 copy-start.4
  41.4 1.2 convolution_convert_fusion.4
  42.7 0.1 reshape.276
  42.7 0.4 fusion.71
  43.1 0.2 copy.54
  43.4 1.4 fusion.27
  44.7 0.0 all-gather.11.cloned.1.call-update
  44.7 0.0 all-gather.13.cloned.1.call-start
  44.8 0.0 copy-start.17
  44.8 14.2 %all-gather.9.cloned.1.call-done = bf16[256,4096]{1,0:T(8,128)(2,1)} async-done(((bf16[256,1024]{1,0:T(8,128)(2,1)}), bf16[256,4096]{1,0:T(8,128)(2,1)}) %all-gather.9.cloned.1.call-update) | async-done | bytes 2097168 | tf_op jit(solution)/shard_map/all_gather | solution.py:58
  59.1 6.4 %convolution_convert_fusion.1 = bf16[256,1024]{1,0:T(8,128)(2,1)S(1)} fusion(bf16[256,4096]{1,0:T(8,128)(2,1)} %all-gather.9.cloned.1.call-done, bf16[1024,4096]{1,0:T(8,128)(2,1)} %param.10), kind=kOutput, calls=%fused_computation.32 | convolution fusion | flops 2147745792 | bytes 11010048 | tf_op jit(solution)/shard_map/dot_general | solution.py:61
  65.5 0.2 copy.56
  65.7 1.3 fusion.26
  67.0 0.0 all-gather.13.cloned.1.call-update
  67.0 0.0 reduce-scatter.3.cloned.1.call-start
  67.1 0.1 mul.221
  67.2 0.1 mul.222
  67.2 0.7 mul.223
  67.9 20.6 %all_gather.16 = bf16[8,2,8]{2,1,0:T(2,128)(2,1)S(1)} all-gather(bf16[1,2,8]{2,1,0:T(2,128)(2,1)S(1)} %get-tuple-element.180), channel_id=1, replica_groups=mesh['seq'=8,'head'=4] {'seq'}, dimensions={0}, use_global_device_ids=true | all-gather | bytes 288 | tf_op jit(solution)/shard_map/all_gather | solution.py:91
  88.6 0.1 fusion.65
  88.7 0.6 sqrt_bitcast_fusion
  89.3 1.0 copy.52
  90.3 0.2 fusion.55
  90.6 0.8 copy-done.9
  91.3 4.6 %fusion.15 = f32[256,2,8,64]{0,3,2,1:T(8,128)S(1)} fusion(bf16[256,2,8,64]{0,3,2,1:T(8,128)(2,1)} %bitcast.157, f32[2,8,256]{2,1,0:T(8,128)} %sqrt_bitcast_fusion, f32[2,8,256]{2,1,0:T(8,128)S(1)} %get-tuple-element.173, f32[2,256,256]{2,1,0:T(8,128)S(1)} %fusion.55, pred[256,256]{1,0:T(8,128)(4,1)S(1)} %iota_compare_fusion), kind=kOutput, calls=%fused_computation.22 | convolution fusion | flops 810549248 | bytes 2195456 | tf_op jit(solution)/shard_map/jvp()/while/body/eval_jaxpr/ghts,sghp->tghp/dot_general | solution.py:23
  95.9 0.6 fusion.21
  96.5 1.3 copy.53
  97.8 12.8 %all-gather.11.cloned.1.call-done = bf16[16,8,128,64]{2,3,1,0:T(8,128)(2,1)} async-done(((bf16[2,8,128,64]{2,3,1,0:T(8,128)(2,1)}), bf16[16,8,128,64]{2,3,1,0:T(8,128)(2,1)}) %all-gather.11.cloned.1.call-update) | async-done | bytes 2097168 | tf_op jit(solution)/shard_map/all_gather | solution.py:94
  110.6 2.1 multiply_reduce_fusion.1
  112.7 1.6 fusion.19
  114.3 2.5 %copy.55 = f32[256,1024]{1,0:T(8,128)} copy(f32[256,1024]{0,1:T(8,128)} %bitcast.153) | data formatting | bytes 2097152 | tf_op jit(solution)/shard_map/jvp()/reshape | solution.py:121
  116.9 8.2 %convolution_convert_fusion = bf16[256,4096]{1,0:T(8,128)(2,1)} fusion(bf16[1024,4096]{1,0:T(8,128)(2,1)} %param.10, f32[256,1024]{1,0:T(8,128)} %copy.55, f32[256,1024]{1,0:T(8,128)} %copy.53, f32[1024]{0:T(1024)S(1)} %copy-done.14, bf16[256,1024]{1,0:T(8,128)(2,1)} %copy-done.4), kind=kOutput, calls=%fused_computation.2 | convolution fusion | flops 2149842944 | bytes 13111296 | tf_op jit(solution)/shard_map/dot_general | solution.py:125
  125.0 0.0 reduce-scatter.3.cloned.1.call-update
  125.1 0.3 reduce-scatter.5.cloned.1.call-start
  125.3 1.0 copy.57
  126.4 0.8 convolution_bitcast_fusion.6
  127.2 2.9 %multiply_reduce_fusion.2 = f32[2,256,256]{2,1,0:T(8,128)S(1)} fusion(bf16[2,8,64,256]{3,2,1,0:T(8,128)(2,1)} %bitcast.159, bf16[256,2,8,64]{0,3,2,1:T(8,128)(2,1)} %bitcast.158, f32[2,8,256]{2,1,0:T(8,128)S(1)} %copy-done.13, f32[2,8,256]{2,1,0:T(8,128)S(1)} %get-tuple-element.173, pred[256,256]{1,0:T(8,128)(4,1)S(1)} %iota_compare_fusion), kind=kOutput, calls=%fused_computation.5 | convolution fusion | flops 140378112 | bytes 1671168 | tf_op jit(solution)/shard_map/transpose(jvp())/while/body/eval_jaxpr/ghts,sghp->tghp/dot_general | solution.py:23
  130.1 0.8 copy-done.5
  130.9 1.2 fusion.25
  132.1 3.9 %fusion.16 = f32[256,2,8,64]{0,3,2,1:T(8,128)} fusion(bf16[2,8,64,256]{3,2,1,0:T(8,128)(2,1)S(1)} %bitcast.160, f32[2,8,256]{2,1,0:T(8,128)S(1)} %copy-done.13, f32[2,8,256]{2,1,0:T(8,128)S(1)} %get-tuple-element.173, f32[2,256,256]{2,1,0:T(8,128)S(1)} %copy-done.10, pred[256,256]{1,0:T(8,128)(4,1)S(1)} %iota_compare_fusion), kind=kOutput, calls=%fused_computation.23 | convolution fusion | flops 810549248 | bytes 2195456 | tf_op jit(solution)/shard_map/transpose(jvp())/while/body/eval_jaxpr/ghts,sghp->tghp/dot_general | solution.py:23
  135.9 24.8 %all-gather.13.cloned.1.call-done = bf16[16,8,128,64]{2,3,1,0:T(8,128)(2,1)} async-done(((bf16[2,8,128,64]{2,3,1,0:T(8,128)(2,1)}), bf16[16,8,128,64]{2,3,1,0:T(8,128)(2,1)}) %all-gather.13.cloned.1.call-update) | async-done | bytes 2097168 | tf_op jit(solution)/shard_map/all_gather | solution.py:97
  160.7 2.2 multiply_reduce_fusion
  163.0 1.1 convolution_bitcast_fusion.5
  164.1 0.4 fusion.24
  164.5 1.1 convolution_bitcast_fusion.4
  165.7 0.6 fusion.18
  166.3 0.3 copy.58
  166.7 6.6 %fusion.35 = f32[256,4096]{1,0:T(8,128)S(1)} fusion(bf16[4096,1024]{1,0:T(8,128)(2,1)} %param.8, f32[256,1024]{1,0:T(8,128)S(1)} %copy.58, f32[1024]{0:T(1024)S(1)} %copy-done.15, bf16[256,1024]{1,0:T(8,128)(2,1)S(1)} %copy-done.3), kind=kOutput, calls=%fused_computation.57 | convolution fusion | flops 2148532224 | bytes 14159872 | tf_op jit(solution)/shard_map/dot_general | solution.py:131
  173.3 2.6 %fusion = bf16[256,4096]{1,0:T(8,128)(2,1)} fusion(f32[256,4096]{1,0:T(8,128)S(1)} %fusion.35, bf16[256,512]{0,1:T(8,128)(2,1)S(1)} %bitcast.156, bf16[4096,512]{1,0:T(8,128)(2,1)S(1)} %copy-done.1), kind=kOutput, calls=%fused_computation.1 | convolution fusion | flops 1075838976 | bytes 10747904 | tf_op jit(solution)/shard_map/dot_general | solution.py:137
  175.9 0.0 reduce-scatter.5.cloned.1.call-update
  176.0 17.7 %reduce-scatter.3.cloned.1.call-done = bf16[256,1024]{1,0:T(8,128)(2,1)} async-done(((bf16[256,4096]{1,0:T(8,128)(2,1)}), bf16[256,1024]{1,0:T(8,128)(2,1)}) %reduce-scatter.3.cloned.1.call-update) | async-done | bytes 524304 | tf_op jit(solution)/shard_map/reduce_scatter | solution.py:126
  193.6 34.6 %reduce-scatter.5.cloned.1.call-done = bf16[256,1024]{1,0:T(8,128)(2,1)} async-done(((bf16[256,4096]{1,0:T(8,128)(2,1)}), bf16[256,1024]{1,0:T(8,128)(2,1)}) %reduce-scatter.5.cloned.1.call-update) | async-done | bytes 524304 | tf_op jit(solution)/shard_map/reduce_scatter | solution.py:143
  (43 shorter events, 0.3 us)
Async XLA Ops:
  7.2 27.7 %all-gather.7.cloned.1.call-start = ((), (), s32[]{:S(2)}) async-start(), calls=%async_computation.2 | async-start | bytes 2621440 | tf_op jit(solution)/shard_map/all_gather | solution.py:57
  7.9 51.2 %all-gather.9.cloned.1.call-start = ((), (), s32[]{:S(2)}) async-start(), calls=%async_computation.4 | async-start | bytes 2621440 | tf_op jit(solution)/shard_map/all_gather | solution.py:58
  8.6 102.0 %all-gather.11.cloned.1.call-start = ((), (), s32[]{:S(2)}) async-start(), calls=%async_computation.6 | async-start | bytes 2359296 | tf_op jit(solution)/shard_map/all_gather | solution.py:94
  34.9 6.5 %copy-start = (bf16[4096,512]{1,0:T(8,128)(2,1)S(1)}, bf16[4096,512]{1,0:T(8,128)(2,1)}, u32[]{:S(2)}) copy-start(bf16[4096,512]{1,0:T(8,128)(2,1)} %param.9) | copy-start | bytes 12582916
  34.9 6.5 %copy-start.16 = (bf16[256,4096]{1,0:T(8,128)(2,1)S(1)}, bf16[256,4096]{1,0:T(8,128)(2,1)}, u32[]{:S(2)}) copy-start(bf16[256,4096]{1,0:T(8,128)(2,1)} %all-gather.7.cloned.1.call-done) | copy-start | bytes 6291460
  41.4 47.9 %copy-start.4 = (bf16[256,1024]{1,0:T(8,128)(2,1)}, bf16[256,1024]{1,0:T(8,128)(2,1)S(1)}, u32[]{:S(2)}) copy-start(bf16[256,1024]{1,0:T(8,128)(2,1)S(1)} %convolution_convert_fusion.2) | copy-start | bytes 1572868
  44.7 116.0 %all-gather.13.cloned.1.call-start = ((), (), s32[]{:S(2)}) async-start(), calls=%async_computation.7 | async-start | bytes 2359296 | tf_op jit(solution)/shard_map/all_gather | solution.py:97
  44.8 22.3 %copy-start.17 = (f32[16]{0:T(128)S(1)}, f32[16]{0:T(128)}, u32[]{:S(2)}) copy-start(f32[16]{0:T(128)} %param.12) | copy-start | bytes 196
  44.8 43.9 %copy-start.12 = (f32[16,256]{1,0:T(8,128)S(1)}, f32[16,256]{1,0:T(8,128)}, u32[]{:S(2)}) copy-start(f32[16,256]{1,0:T(8,128)} %param.11) | copy-start | bytes 49156
  65.5 25.1 %copy-start.2 = (bf16[256,1024]{1,0:T(8,128)(2,1)}, bf16[256,1024]{1,0:T(8,128)(2,1)S(1)}, u32[]{:S(2)}) copy-start(bf16[256,1024]{1,0:T(8,128)(2,1)S(1)} %convolution_convert_fusion.1) | copy-start | bytes 1572868
  67.0 126.6 %reduce-scatter.3.cloned.1.call-start = ((), (), s32[]{:S(2)}) async-start(), calls=%async_computation.3 | async-start | bytes 2621440 | tf_op jit(solution)/shard_map/reduce_scatter | solution.py:126
  90.6 0.8 copy-start.9
  96.5 20.3 %copy-start.14 = (f32[1024]{0:T(1024)S(1)}, f32[1024]{0:T(1024)}, u32[]{:S(2)}) copy-start(f32[1024]{0:T(1024)} %mul.223) | copy-start | bytes 12292
  116.9 8.5 %copy-start.3 = (bf16[256,1024]{1,0:T(8,128)(2,1)S(1)}, bf16[256,1024]{1,0:T(8,128)(2,1)}, u32[]{:S(2)}) copy-start(bf16[256,1024]{1,0:T(8,128)(2,1)} %copy-done.2) | copy-start | bytes 1572868
  125.0 2.1 copy-start.13
  125.1 103.2 %reduce-scatter.5.cloned.1.call-start = ((), (), s32[]{:S(2)}) async-start(), calls=%async_computation.5 | async-start | bytes 2621440 | tf_op jit(solution)/shard_map/reduce_scatter | solution.py:143
  127.1 4.9 %copy-start.10 = (f32[2,256,256]{2,1,0:T(8,128)S(1)}, f32[2,256,256]{2,1,0:T(8,128)}, u32[]{:S(2)}) copy-start(f32[2,256,256]{2,1,0:T(8,128)} %copy-done.9) | copy-start | bytes 1572868
  127.1 4.9 %copy-start.11 = (bf16[256,1024]{0,1:T(8,128)(2,1)S(1)}, bf16[256,1024]{0,1:T(8,128)(2,1)}, u32[]{:S(2)}) copy-start(bf16[256,1024]{0,1:T(8,128)(2,1)} %copy.57) | copy-start | bytes 1572868
  130.1 0.8 copy-start.5
  160.7 3.4 %copy-start.6 = (f32[2,256,256]{2,1,0:T(8,128)S(1)}, f32[2,256,256]{2,1,0:T(8,128)}, u32[]{:S(2)}) copy-start(f32[2,256,256]{2,1,0:T(8,128)} %copy-done.5) | copy-start | bytes 1572868
  160.7 4.9 %copy-start.8 = (f32[256,2,1,128]{0,3,1,2:T(8,128)S(1)}, f32[256,2,1,128]{0,3,1,2:T(8,128)}, u32[]{:S(2)}) copy-start(f32[256,2,1,128]{0,3,1,2:T(8,128)} %fusion.25) | copy-start | bytes 786436
  160.7 5.0 %copy-start.7 = (f32[256,2,8,64]{0,3,2,1:T(8,128)S(1)}, f32[256,2,8,64]{0,3,2,1:T(8,128)}, u32[]{:S(2)}) copy-start(f32[256,2,8,64]{0,3,2,1:T(8,128)} %fusion.16) | copy-start | bytes 3145732
  164.5 2.2 copy-start.15
  166.7 6.6 %copy-start.1 = (bf16[4096,512]{1,0:T(8,128)(2,1)S(1)}, bf16[4096,512]{1,0:T(8,128)(2,1)}, u32[]{:S(2)}) copy-start(bf16[4096,512]{1,0:T(8,128)(2,1)} %param.9) | copy-start | bytes 12582916
Sparse Core Ops, SparseCore 0:
  9.6 25.2 all-gather.6
  36.4 22.5 all-gather.8
  61.2 49.3 all-gather.10
  112.6 48.0 all-gather.12
  163.7 29.9 reduce-scatter.2
  196.8 31.4 reduce-scatter.4
where the time goes:
time: 235 us
  waiting for transfers between devices  128 us (54%)
  matrix products  53.1 us (23%)
  blocking collectives  20.6 us (9%)
  between operations  14.5 us (6%)
  local copies, waits for them, and re-layouts  9.86 us (4%)
  other arithmetic  8.28 us (4%)
    reduce_scatter x1, waiting for transfers between devices, per_device(): lax.psum_scatter(partial_grad.astype(jnp.bfloat16), 'head', scatter_dimen...  34.6 us
    all_gather x1, waiting for transfers between devices, per_device(): lax.all_gather(grad_state[None].astype(jnp.bfloat16), 'seq', axis=0, tile...  24.8 us
    all_gather x1, waiting for transfers between devices, per_device(): input_piece = lax.all_gather(layer_input, 'head', axis=1, tiled=True)  22.7 us
    all_gather x1, blocking collectives, per_device(): lax.all_gather(decay_total[None].astype(jnp.bfloat16), 'seq', axis=0, til...  20.6 us
    reduce_scatter x1, waiting for transfers between devices, per_device(): lax.psum_scatter(partial_output.astype(jnp.bfloat16), 'head', scatter_dim...  17.7 us
    all_gather x1, waiting for transfers between devices, per_device(): grad_piece = lax.all_gather(output_grad, 'head', axis=1, tiled=True)  14.2 us
    all_gather x1, waiting for transfers between devices, per_device(): lax.all_gather(end_state[None].astype(jnp.bfloat16), 'seq', axis=0, tiled...  12.8 us
    dot_general x3, matrix products, block_step(): within = jnp.einsum('ghts,sghp->tghp', weights, values, precision=highest)  11.4 us
  transfers between devices with their start and end apart: 6, of which 6 were waited for; matrix products, arithmetic and copies ran while one was open for 30% of the time, Pallas kernels for 0%

commit v1 on v0

v1 whole, which is shorter than its diff:
```python
import functools

import jax
import jax.numpy as jnp
from jax import lax
from jax.experimental import pallas as pl
from jax.experimental.pallas import tpu as pltpu

STATE = 128
TILE = 256
CHUNKS = 2
SEMS = 128
f32 = jnp.float32
bf16 = jnp.bfloat16
HIGHEST = lax.Precision.HIGHEST
MESH = pl.DeviceIdType.MESH


def nn(a, b, precision=None):
    return lax.dot_general(a, b, (((1,), (0,)), ((), ())), precision=precision, preferred_element_type=f32)


def nt(a, b, precision=None):
    return lax.dot_general(a, b, (((1,), (1,)), ((), ())), precision=precision, preferred_element_type=f32)


def tn(a, b):
    return lax.dot_general(a, b, (((0,), (0,)), ((), ())), preferred_element_type=f32)


def inflow_of(decay):
    twice = 2.0 * decay
    series = 1.0 + twice * (1.0 / 9.0)
    for n in (8, 7, 6, 5, 4, 3, 2):
        series = 1.0 + twice * series * (1.0 / n)
    near = -twice * series
    far = 1.0 - jnp.exp(twice)
    return jnp.sqrt(jnp.where(twice > -0.5, near, far))


def kernel(
    n_head, n_seq,
    x_ref, g_ref, ld_ref, skip_ref, vw_hbm, sw_hbm, ow_hbm,
    out_ref, ing_ref,
    vw, sw, ow, xs, gs, acc_v, acc_p, acc_g, values, pairs, mgrad, mix, dval, dpair,
    ent_x, end_x, run_x, run_r, inf_r, score, dscore, tv, eg,
    total, excl, dtot, dexc, sendb, recvb, sendd, recvd,
    p_send, p_recv, y_send, y_recv, o_send, o_recv, part,
    ssem, rsem, wsem,
):
    rows, width = x_ref.shape
    vwid = vw.shape[1]
    pwid = sw.shape[1]
    heads = ld_ref.shape[0]
    groups = pwid // (2 * STATE)
    gwid = vwid // groups
    hdim = vwid // heads
    pair = 2 * hdim
    chips = n_head // 2
    steps = recvb.shape[1]
    hi = lax.axis_index("head")
    si = lax.axis_index("seq")
    core = lax.rem(hi, 2)
    chip = hi // 2
    partner = chip * 2 + (1 - core)

    def at_chip(j, c):
        return lax.rem(chip + j, chips) * 2 + c

    barrier = pltpu.get_barrier_semaphore()
    peers = [{"head": partner}] + [{"head": at_chip(j, core)} for j in range(1, chips)]
    offsets = set()
    for k in range(steps):
        offsets |= {2**k % n_seq, (n_seq - 2**k) % n_seq}
    offsets.discard(0)
    peers += [{"seq": lax.rem(si + o, n_seq)} for o in sorted(offsets)]

    counter = [0]

    def remote(src, dst, device):
        i = counter[0]
        counter[0] += 1
        return pltpu.make_async_remote_copy(
            src_ref=src, dst_ref=dst, send_sem=ssem.at[i], recv_sem=rsem.at[i],
            device_id=device, device_id_type=MESH,
        )

    order = [hi, partner]
    for j in range(1, chips):
        order += [at_chip(chips - j, core), at_chip(chips - j, 1 - core)]
    wcopies = []
    wcount = 0
    for src in order:
        at = pl.ds(pl.multiple_of(src * width, width), width)
        three = []
        for a, b in (
            (vw_hbm.at[at, :], vw.at[at, :]),
            (sw_hbm.at[at, :], sw.at[at, :]),
            (ow_hbm.at[:, at], ow.at[:, at]),
        ):
            three.append(pltpu.make_async_copy(a, b, wsem.at[wcount]))
            wcount += 1
        wcopies.append(three)
    for three in wcopies:
        three[0].start()
        three[1].start()

    for peer in peers:
        pl.semaphore_signal(barrier, inc=1, device_id=peer, device_id_type=MESH)
    pl.semaphore_wait(barrier, len(peers))

    crow = rows // CHUNKS

    def gather(t_ref, slots):
        own = remote(t_ref, slots.at[hi], {"head": partner})
        far, fwd = [], []
        for k in range(CHUNKS):
            at = pl.ds(k * crow, crow)
            for j in range(1, chips):
                far.append(remote(t_ref.at[at], slots.at[hi, at], {"head": at_chip(j, core)}))
                src = at_chip(chips - j, core)
                fwd.append(remote(slots.at[src, at], slots.at[src, at], {"head": partner}))
        return own, far, fwd

    x_own, x_far, x_fwd = gather(x_ref, xs)
    g_own, g_far, g_fwd = gather(g_ref, gs)
    for c in x_far:
        c.start()
    x_own.start()
    g_own.start()
    for three in wcopies:
        three[2].start()

    decay = ld_ref[...]
    ti = lax.broadcasted_iota(jnp.int32, (rows, rows), 0)
    si_ = lax.broadcasted_iota(jnp.int32, (rows, rows), 1)
    lower = jnp.where(ti >= si_, 1.0, 0.0).astype(f32)
    eye = jnp.where(ti == si_, 1.0, 0.0).astype(f32)
    run_row = nt(decay, lower, HIGHEST)
    run_col = nt(lower, decay, HIGHEST)
    decay_col = nt(eye, decay, HIGHEST)
    inf_row = inflow_of(decay)
    for h in range(heads):
        run_r[h] = run_row[h : h + 1, :]
        inf_r[h] = inf_row[h : h + 1, :]
    col = lax.broadcasted_iota(jnp.int32, (heads, vwid), 1)
    first = lax.broadcasted_iota(jnp.int32, (heads, vwid), 0) * hdim
    spread = jnp.where((col >= first) & (col < first + hdim), 1.0, 0.0).astype(f32)
    run_x[...] = nn(run_col, spread, HIGHEST)
    ent_x[...] = nn(jnp.exp(run_col), spread, HIGHEST)
    to_end = jnp.exp(run_col[rows - 1 : rows, :] - run_col) * inflow_of(decay_col)
    end_x[...] = nn(to_end, spread, HIGHEST)

    def mul_x(src, block, begin):
        @pl.loop(0, vwid // TILE)
        def _(n):
            at = pl.ds(pl.multiple_of(n * TILE, TILE), TILE)
            p = nn(block[...], vw[pl.ds(pl.multiple_of(src * width, width), width), at])
            acc_v[:, at] = p if begin else acc_v[:, at] + p

        @pl.loop(0, pwid // TILE)
        def _(n):
            at = pl.ds(pl.multiple_of(n * TILE, TILE), TILE)
            p = nn(block[...], sw[pl.ds(pl.multiple_of(src * width, width), width), at])
            acc_p[:, at] = p if begin else acc_p[:, at] + p

    def mul_g(src, block, begin):
        @pl.loop(0, vwid // TILE)
        def _(n):
            at = pl.ds(pl.multiple_of(n * TILE, TILE), TILE)
            p = nt(block[...], ow[at, pl.ds(pl.multiple_of(src * width, width), width)])
            acc_g[:, at] = p if begin else acc_g[:, at] + p

    wcopies[0][0].wait()
    wcopies[0][1].wait()
    mul_x(hi, x_ref, True)
    x_own.wait_recv()
    wcopies[1][0].wait()
    wcopies[1][1].wait()
    mul_x(partner, xs.at[partner], False)
    per = chips - 1
    for k in range(CHUNKS):
        for j in range(per):
            x_far[k * per + j].wait_recv()
            x_fwd[k * per + j].start()
            g_far[k * per + j].start()
    wcopies[0][2].wait()
    mul_g(hi, g_ref, True)
    for j in range(per):
        src = at_chip(chips - 1 - j, core)
        for which in (0, 1):
            wcopies[2 + 2 * j + which][0].wait()
            wcopies[2 + 2 * j + which][1].wait()
        mul_x(src, xs.at[src], False)
        for k in range(CHUNKS):
            x_fwd[k * per + j].wait_recv()
        src = at_chip(chips - 1 - j, 1 - core)
        mul_x(src, xs.at[src], False)
    values[...] = acc_v[...].astype(bf16)
    pairs[...] = acc_p[...].astype(bf16)

    copies = []
    for way in (0, 1):
        for k in range(steps):
            hop = 2**k
            to = si + hop if way == 0 else si - hop
            to = lax.rem(to + n_seq, n_seq)
            a = remote(sendb.at[way, k], recvb.at[way, k], {"seq": to})
            b = remote(sendd.at[way, k], recvd.at[way, k], {"seq": to})
            copies.append((a, b))

    def can_send(way, k):
        return si + 2**k < n_seq if way == 0 else si >= 2**k

    def can_recv(way, k):
        return si >= 2**k if way == 0 else si + 2**k < n_seq

    def scan_send(way, k):
        sendb[way, k] = total[way].astype(bf16)
        sendd[way, k] = dtot[way]

        @pl.when(can_send(way, k))
        def _():
            for c in copies[way * steps + k]:
                c.start()

    def scan_take(way, k):
        @pl.when(can_recv(way, k))
        def _():
            for c in copies[way * steps + k]:
                c.wait_recv()
            got = recvb[way, k].astype(f32)
            excl[way] = excl[way] + dexc[way][0:1, :] * got
            if k < steps - 1:
                total[way] = total[way] + dtot[way][0:1, :] * got
                dexc[way] = dexc[way] * recvd[way, k]
                dtot[way] = dtot[way] * recvd[way, k]

        if k < steps - 1:
            scan_send(way, k + 1)

    def scan_begin(way):
        excl[way] = jnp.zeros(excl.shape[1:], f32)
        dexc[way] = jnp.ones(dexc.shape[1:], f32)
        dtot[way] = jnp.broadcast_to(ent_x[rows - 1 : rows, :], dtot.shape[1:])
        if steps > 0:
            scan_send(way, 0)

    tv[...] = (end_x[...] * values[...].astype(f32)).astype(bf16)
    for g in range(groups):
        cols = slice(g * gwid, (g + 1) * gwid)
        w_at = slice(2 * g * STATE, (2 * g + 1) * STATE)
        total[0, :, cols] = tn(pairs[:, w_at], tv[:, cols])
    scan_begin(0)
    for g in range(groups):
        w_at = slice(2 * g * STATE, (2 * g + 1) * STATE)
        r_at = slice((2 * g + 1) * STATE, (2 * g + 2) * STATE)
        score[g] = nt(pairs[:, r_at], pairs[:, w_at])
        dscore[g] = jnp.zeros((rows, rows), f32)

    g_own.wait_recv()
    wcopies[1][2].wait()
    mul_g(partner, gs.at[partner], False)
    for k in range(CHUNKS):
        for j in range(per):
            g_far[k * per + j].wait_recv()
            g_fwd[k * per + j].start()
    for j in range(per):
        src = at_chip(chips - 1 - j, core)
        for which in (0, 1):
            wcopies[2 + 2 * j + which][2].wait()
        mul_g(src, gs.at[src], False)
        for k in range(CHUNKS):
            g_fwd[k * per + j].wait_recv()
        src = at_chip(chips - 1 - j, 1 - core)
        mul_g(src, gs.at[src], False)
    mgrad[...] = acc_g[...].astype(bf16)
    eg[...] = (ent_x[...] * mgrad[...].astype(f32)).astype(bf16)
    for g in range(groups):
        cols = slice(g * gwid, (g + 1) * gwid)
        r_at = slice((2 * g + 1) * STATE, (2 * g + 2) * STATE)
        total[1, :, cols] = tn(pairs[:, r_at], eg[:, cols])
    scan_begin(1)

    per_group = gwid // pair

    def within(begin, end):
        @pl.loop(begin, end)
        def _(i):
            g = i // per_group
            at = pl.ds(pl.multiple_of(i * pair, pair), pair)
            left = lax.broadcasted_iota(jnp.int32, (rows, pair), 1) < hdim
            causal = lax.broadcasted_iota(jnp.int32, (rows, rows), 0) >= lax.broadcasted_iota(
                jnp.int32, (rows, rows), 1
            )
            vp = values[:, at]
            gp = mgrad[:, at]
            gp32 = gp.astype(f32)
            rx = run_x[:, at]
            s = score[g]
            gain = jnp.where(left, skip_ref[2 * i], skip_ref[2 * i + 1])
            outs, grads, ds = [], [], None
            for h in (0, 1):
                rc = rx[:, h * hdim : h * hdim + 1]
                m = jnp.exp(jnp.where(causal, rc - run_r[2 * i + h], -1e30)) * inf_r[2 * i + h]
                w = (s * m).astype(bf16)
                outs.append(nn(w, vp))
                grads.append(tn(w, gp))
                gh = jnp.where(left == (h == 0), gp32, 0.0).astype(bf16)
                d = m * nt(gh, vp)
                ds = d if ds is None else ds + d
            acc_v[:, at] = jnp.where(left, outs[0], outs[1]) + gain * vp.astype(f32)
            acc_g[:, at] = jnp.where(left, grads[0], grads[1]) + gain * gp32
            dscore[g] = dscore[g] + ds

    n_pairs = heads // 2
    done = 0
    for k in range(steps):
        scan_take(0, k)
        nxt = (n_pairs * (k + 1)) // max(steps, 1) if k < steps - 1 else n_pairs
        if k < steps - 1 or done < n_pairs:
            within(done, nxt)
            done = nxt
        if k < steps - 1:
            scan_take(1, k)

    def tiles(partial, dest, use):
        @pl.loop(0, width // TILE)
        def _(n):
            use(pl.ds(pl.multiple_of(n * TILE, TILE), TILE), partial(dest * width + n * TILE))

    def scatter_copies(u):
        near = [
            remote(p_send.at[u, j], p_recv.at[u, j], {"head": partner}) for j in range(per)
        ]
        far = [
            remote(y_send.at[u, j], y_recv.at[u, j], {"head": at_chip(j + 1, core)})
            for j in range(per)
        ]
        own = remote(o_send.at[u], o_recv.at[u], {"head": partner})
        return near, far, own

    def scatter_begin(u, partial):
        near, far, own = scatter_copies(u)
        for j in range(per):
            def keep(at, p):
                p_send[u, j, :, at] = p.astype(bf16)

            tiles(partial, at_chip(j + 1, 1 - core), keep)
            near[j].start()
        for j in range(per):
            def keep_part(at, p):
                part[u, :, at] = p

            tiles(partial, at_chip(j + 1, core), keep_part)
            near[j].wait_recv()
            y_send[u, j] = (part[u] + p_recv[u, j].astype(f32)).astype(bf16)
            far[j].start()

        def keep_own(at, p):
            o_send[u, :, at] = p.astype(bf16)

        tiles(partial, partner, keep_own)
        own.start()

        def keep_mine(at, p):
            part[u, :, at] = p

        tiles(partial, hi, keep_mine)
        return near, far, own

    def scatter_end(u, three, o_ref):
        near, far, own = three
        own.wait_recv()
        s = part[u] + o_recv[u].astype(f32)
        for j in range(per):
            far[j].wait_recv()
            s = s + y_recv[u, j].astype(f32)
        o_ref[...] = s.astype(bf16)
        for c in near + far + [own]:
            c.wait_send()

    for g in range(groups):
        cols = slice(g * gwid, (g + 1) * gwid)
        r_at = slice((2 * g + 1) * STATE, (2 * g + 2) * STATE)
        carried = ent_x[:, cols] * nn(pairs[:, r_at], excl[0, :, cols].astype(bf16))
        mix[:, cols] = (acc_v[:, cols] + carried).astype(bf16)

    def out_partial(first_col):
        return nn(mix[...], ow[:, pl.ds(pl.multiple_of(first_col, TILE), TILE)])

    first_rs = scatter_begin(0, out_partial)

    if steps > 0:
        scan_take(1, steps - 1)
    for g in range(groups):
        cols = slice(g * gwid, (g + 1) * gwid)
        w_at = slice(2 * g * STATE, (2 * g + 1) * STATE)
        r_at = slice((2 * g + 1) * STATE, (2 * g + 2) * STATE)
        inc = excl[0, :, cols].astype(bf16)
        outg = excl[1, :, cols].astype(bf16)
        dval[:, cols] = (acc_g[:, cols] + end_x[:, cols] * nn(pairs[:, w_at], outg)).astype(bf16)
        ds = dscore[g].astype(bf16)
        dpair[:, w_at] = (tn(ds, pairs[:, r_at]) + nt(tv[:, cols], outg)).astype(bf16)
        dpair[:, r_at] = (nn(ds, pairs[:, w_at]) + nt(eg[:, cols], inc)).astype(bf16)

    def in_partial(first_row):
        at = pl.ds(pl.multiple_of(first_row, TILE), TILE)
        return nt(dval[...], vw[at, :]) + nt(dpair[...], sw[at, :])

    second_rs = scatter_begin(1, in_partial)
    scatter_end(0, first_rs, out_ref)
    scatter_end(1, second_rs, ing_ref)

    for c in [x_own, g_own] + x_far + x_fwd + g_far + g_fwd:
        c.wait_send()
    for way in (0, 1):
        for k in range(steps):
            @pl.when(can_send(way, k))
            def _():
                for c in copies[way * steps + k]:
                    c.wait_send()


def per_device(
    n_head, n_seq,
    layer_input, value_weight, state_weight, output_weight, log_decay, skip_gain, output_grad,
):
    rows, width = layer_input.shape
    full, vwid = value_weight.shape
    pwid = state_weight.shape[1]
    heads = log_decay.shape[0]
    groups = pwid // (2 * STATE)
    steps = max(n_seq - 1, 0).bit_length()
    chips = n_head // 2
    per = max(chips - 1, 1)
    vm = pltpu.VMEM
    scratch = [
        vm((full, vwid), bf16), vm((full, pwid), bf16), vm((vwid, full), bf16),
        vm((n_head, rows, width), bf16), vm((n_head, rows, width), bf16),
        vm((rows, vwid), f32), vm((rows, pwid), f32), vm((rows, vwid), f32),
        vm((rows, vwid), bf16), vm((rows, pwid), bf16), vm((rows, vwid), bf16),
        vm((rows, vwid), bf16), vm((rows, vwid), bf16), vm((rows, pwid), bf16),
        vm((rows, vwid), f32), vm((rows, vwid), f32), vm((rows, vwid), f32),
        vm((heads, 1, rows), f32), vm((heads, 1, rows), f32),
        vm((groups, rows, rows), f32), vm((groups, rows, rows), f32),
        vm((rows, vwid), bf16), vm((rows, vwid), bf16),
        vm((2, STATE, vwid), f32), vm((2, STATE, vwid), f32),
        vm((2, 8, vwid), f32), vm((2, 8, vwid), f32),
        vm((2, steps, STATE, vwid), bf16), vm((2, steps, STATE, vwid), bf16),
        vm((2, steps, 8, vwid), f32), vm((2, steps, 8, vwid), f32),
        vm((2, per, rows, width), bf16), vm((2, per, rows, width), bf16),
        vm((2, per, rows, width), bf16), vm((2, per, rows, width), bf16),
        vm((2, rows, width), bf16), vm((2, rows, width), bf16),
        vm((2, rows, width), f32),
        pltpu.SemaphoreType.DMA((SEMS,)),
        pltpu.SemaphoreType.DMA((SEMS,)),
        pltpu.SemaphoreType.DMA((3 * n_head,)),
    ]
    vspec = pl.BlockSpec(memory_space=vm)
    anys = pl.BlockSpec(memory_space=pl.ANY)
    flops = 2 * rows * full * (3 * vwid + pwid) + 2 * rows * full * (vwid + pwid)
    return pl.pallas_call(
        functools.partial(kernel, n_head, n_seq),
        out_shape=(
            jax.ShapeDtypeStruct((rows, width), bf16),
            jax.ShapeDtypeStruct((rows, width), bf16),
        ),
        in_specs=[vspec, vspec, vspec, pl.BlockSpec(memory_space=pltpu.SMEM), anys, anys, anys],
        out_specs=(vspec, vspec),
        scratch_shapes=scratch,
        compiler_params=pltpu.CompilerParams(
            collective_id=0, has_side_effects=True, vmem_limit_bytes=60 * 2**20
        ),
        cost_estimate=pl.CostEstimate(
            flops=flops, bytes_accessed=2 * full * (2 * vwid + pwid), transcendentals=0
        ),
    )(layer_input, output_grad, log_decay, skip_gain, value_weight, state_weight, output_weight)


def solution(mesh):
    from jax.sharding import PartitionSpec as P

    in_specs = (
        P("seq", "head"),
        P(None, "head"),
        P(None, "head"),
        P("head", None),
        P("head", "seq"),
        P("head"),
        P("seq", "head"),
    )
    out_specs = (P("seq", "head"), P("seq", "head"))
    return jax.shard_map(
        functools.partial(per_device, mesh.shape["head"], mesh.shape["seq"]),
        mesh=mesh, in_specs=in_specs, out_specs=out_specs, check_vma=False,
    )
```

time: 235 us -> 92.4 us (0.39)
  the two profiles are of different devices: /device:TPU:0 before, /device:TPU:11 now
where the time goes in v1:
time: 92.4 us; the launch traced here: 92.2 us
  Pallas kernels  87.8 us (95%)
  local copies, waits for them, and re-layouts  3.74 us (4%)
    pallas_call x1, Pallas kernels, per_device(): pl.pallas_call(functools.partial(kernel, n_head, n_seq), out_shape=(jax.S...  87.8 us
    unnamed x2, local copies, waits for them, and re-layouts  3.74 us

profile of v1, /device:TPU:11, one launch (start us, length us, event | category | flops | bytes accessed | tf_op | source)
XLA Modules:
  0.0 92.2 jit_solution(11506249776145794235)
XLA Ops:
  0.6 87.8 %shard_map.86 = (bf16[256,1024]{1,0:T(8,128)(2,1)}, bf16[256,1024]{1,0:T(8,128)(2,1)}) custom-call(bf16[256,1024]{1,0:T(8,128)(2,1)} %x_ref.1, bf16[256,1024]{1,0:T(8,128)(2,1)} %g_ref.1, f32[16,256]{1,0:T(8,128)} %ld_ref.1, f32[16]{0:T(128)} %skip_ref.1, bf16[4096,1024]{1,0:T(8,128)(2,1)} %vw_hbm.1, bf16[4096,512]{1,0:T(8,128)(2,1)} %sw_hbm.1, ...), custom_call_target="tpu_custom_call" | custom-call | flops 10737418240 | bytes 20971520 | tf_op jit(solution)/shard_map/pallas_call | solution.py:463
  88.4 1.9 %copy.11 = bf16[256,1024]{1,0:T(8,128)(2,1)} copy(bf16[256,1024]{1,0:T(8,128)(2,1)} %get-tuple-element.4) | data formatting | bytes 1048576
  90.3 1.9 %copy.12 = bf16[256,1024]{1,0:T(8,128)(2,1)} copy(bf16[256,1024]{1,0:T(8,128)(2,1)} %get-tuple-element.5) | data formatting | bytes 1048576

commit v2 on v1

--- a/solution.py
+++ b/solution.py
@@ -9,7 +9,6 @@
 STATE = 128
 TILE = 256
 CHUNKS = 2
-SEMS = 128
 f32 = jnp.float32
 bf16 = jnp.bfloat16
 HIGHEST = lax.Precision.HIGHEST
@@ -44,7 +43,7 @@
     out_ref, ing_ref,
     vw, sw, ow, xs, gs, acc_v, acc_p, acc_g, values, pairs, mgrad, mix, dval, dpair,
     ent_x, end_x, run_x, run_r, inf_r, score, dscore, tv, eg,
-    total, excl, dtot, dexc, sendb, recvb, sendd, recvd,
+    total, excl, sendb, recvb, backb, backr, sendd, recvd, dec,
     p_send, p_recv, y_send, y_recv, o_send, o_recv, part,
     ssem, rsem, wsem,
 ):
@@ -57,7 +56,9 @@
     hdim = vwid // heads
     pair = 2 * hdim
     chips = n_head // 2
-    steps = recvb.shape[1]
+    row_cuts = min(n_seq, STATE // 16)
+    col_cuts = n_seq // row_cuts
+    prow, pcol = STATE // row_cuts, vwid // col_cuts
     hi = lax.axis_index("head")
     si = lax.axis_index("seq")
     core = lax.rem(hi, 2)
@@ -69,11 +70,7 @@
 
     barrier = pltpu.get_barrier_semaphore()
     peers = [{"head": partner}] + [{"head": at_chip(j, core)} for j in range(1, chips)]
-    offsets = set()
-    for k in range(steps):
-        offsets |= {2**k % n_seq, (n_seq - 2**k) % n_seq}
-    offsets.discard(0)
-    peers += [{"seq": lax.rem(si + o, n_seq)} for o in sorted(offsets)]
+    peers += [{"seq": lax.rem(si + o, n_seq)} for o in range(1, n_seq)]
 
     counter = [0]
 
@@ -150,6 +147,15 @@
     ent_x[...] = nn(jnp.exp(run_col), spread, HIGHEST)
     to_end = jnp.exp(run_col[rows - 1 : rows, :] - run_col) * inflow_of(decay_col)
     end_x[...] = nn(to_end, spread, HIGHEST)
+
+    sendd[...] = jnp.zeros(sendd.shape, f32)
+    sendd[:, 0:heads] = jnp.broadcast_to(jnp.exp(run_col[rows - 1 : rows, :]), (8, heads))
+    recvd[si] = sendd[...]
+    d_copies = [
+        remote(sendd, recvd.at[si], {"seq": lax.rem(si + o, n_seq)}) for o in range(1, n_seq)
+    ]
+    for c in d_copies:
+        c.start()
 
     def mul_x(src, block, begin):
         @pl.loop(0, vwid // TILE)
@@ -199,52 +205,42 @@
     values[...] = acc_v[...].astype(bf16)
     pairs[...] = acc_p[...].astype(bf16)
 
-    copies = []
+    there, back = [], []
     for way in (0, 1):
-        for k in range(steps):
-            hop = 2**k
-            to = si + hop if way == 0 else si - hop
-            to = lax.rem(to + n_seq, n_seq)
-            a = remote(sendb.at[way, k], recvb.at[way, k], {"seq": to})
-            b = remote(sendd.at[way, k], recvd.at[way, k], {"seq": to})
-            copies.append((a, b))
-
-    def can_send(way, k):
-        return si + 2**k < n_seq if way == 0 else si >= 2**k
-
-    def can_recv(way, k):
-        return si >= 2**k if way == 0 else si + 2**k < n_seq
-
-    def scan_send(way, k):
-        sendb[way, k] = total[way].astype(bf16)
-        sendd[way, k] = dtot[way]
-
-        @pl.when(can_send(way, k))
-        def _():
-            for c in copies[way * steps + k]:
-                c.start()
-
-    def scan_take(way, k):
-        @pl.when(can_recv(way, k))
-        def _():
-            for c in copies[way * steps + k]:
-                c.wait_recv()
-            got = recvb[way, k].astype(f32)
-            excl[way] = excl[way] + dexc[way][0:1, :] * got
-            if k < steps - 1:
-                total[way] = total[way] + dtot[way][0:1, :] * got
-                dexc[way] = dexc[way] * recvd[way, k]
-                dtot[way] = dtot[way] * recvd[way, k]
-
-        if k < steps - 1:
-            scan_send(way, k + 1)
+        to = [lax.rem(si + o, n_seq) for o in range(1, n_seq)]
+        there.append([remote(sendb.at[way, t], recvb.at[way, si], {"seq": t}) for t in to])
+        back.append([remote(backb.at[way, t], backr.at[way, si], {"seq": t}) for t in to])
+
+    def piece(r):
+        row, col = (r % row_cuts) * prow, (r // row_cuts) * pcol
+        return slice(row, row + prow), slice(col, col + pcol)
 
     def scan_begin(way):
-        excl[way] = jnp.zeros(excl.shape[1:], f32)
-        dexc[way] = jnp.ones(dexc.shape[1:], f32)
-        dtot[way] = jnp.broadcast_to(ent_x[rows - 1 : rows, :], dtot.shape[1:])
-        if steps > 0:
-            scan_send(way, 0)
+        for r in range(n_seq):
+            at = piece(r)
+            sendb[way, r] = total[way, at[0], at[1]].astype(bf16)
+        for c in there[way]:
+            c.start()
+        recvb[way, si] = sendb[way, si]
+
+    def scan_mid(way):
+        for c in there[way]:
+            c.wait_recv()
+        cols = pl.ds(pl.multiple_of((si // row_cuts) * pcol, 128), pcol)
+        state = jnp.zeros((prow, pcol), f32)
+        for q in range(n_seq) if way == 0 else range(n_seq - 1, -1, -1):
+            backb[way, q] = state.astype(bf16)
+            state = dec[q, 0:1, cols] * state + recvb[way, q].astype(f32)
+        for c in back[way]:
+            c.start()
+        backr[way, si] = backb[way, si]
+
+    def scan_end(way):
+        for c in back[way]:
+            c.wait_recv()
+        for r in range(n_seq):
+            at = piece(r)
+            excl[way, at[0], at[1]] = backr[way, r]
 
     tv[...] = (end_x[...] * values[...].astype(f32)).astype(bf16)
     for g in range(groups):
@@ -252,6 +248,13 @@
         w_at = slice(2 * g * STATE, (2 * g + 1) * STATE)
         total[0, :, cols] = tn(pairs[:, w_at], tv[:, cols])
     scan_begin(0)
+    for c in d_copies:
+        c.wait_recv()
+    lane = lax.broadcasted_iota(jnp.int32, (128, vwid), 1)
+    head = lax.broadcasted_iota(jnp.int32, (128, vwid), 0) * hdim
+    widen = jnp.where((lane >= head) & (lane < head + hdim), 1.0, 0.0).astype(f32)
+    wide = nn(recvd[...].reshape(n_seq * 8, 128), widen, HIGHEST)
+    dec[...] = wide.reshape(n_seq, 8, vwid)
     for g in range(groups):
         w_at = slice(2 * g * STATE, (2 * g + 1) * STATE)
         r_at = slice((2 * g + 1) * STATE, (2 * g + 2) * STATE)
@@ -261,6 +264,7 @@
     g_own.wait_recv()
     wcopies[1][2].wait()
     mul_g(partner, gs.at[partner], False)
+    scan_mid(0)
     for k in range(CHUNKS):
         for j in range(per):
             g_far[k * per + j].wait_recv()
@@ -313,16 +317,8 @@
             acc_g[:, at] = jnp.where(left, grads[0], grads[1]) + gain * gp32
             dscore[g] = dscore[g] + ds
 
-    n_pairs = heads // 2
-    done = 0
-    for k in range(steps):
-        scan_take(0, k)
-        nxt = (n_pairs * (k + 1)) // max(steps, 1) if k < steps - 1 else n_pairs
-        if k < steps - 1 or done < n_pairs:
-            within(done, nxt)
-            done = nxt
-        if k < steps - 1:
-            scan_take(1, k)
+    within(0, heads // 2)
+    scan_end(0)
 
     def tiles(partial, dest, use):
         @pl.loop(0, width // TILE)
@@ -383,7 +379,7 @@
     for g in range(groups):
         cols = slice(g * gwid, (g + 1) * gwid)
         r_at = slice((2 * g + 1) * STATE, (2 * g + 2) * STATE)
-        carried = ent_x[:, cols] * nn(pairs[:, r_at], excl[0, :, cols].astype(bf16))
+        carried = ent_x[:, cols] * nn(pairs[:, r_at], excl[0, :, cols])
         mix[:, cols] = (acc_v[:, cols] + carried).astype(bf16)
 
     def out_partial(first_col):
@@ -391,14 +387,14 @@
 
     first_rs = scatter_begin(0, out_partial)
 
-    if steps > 0:
-        scan_take(1, steps - 1)
+    scan_mid(1)
+    scan_end(1)
     for g in range(groups):
         cols = slice(g * gwid, (g + 1) * gwid)
         w_at = slice(2 * g * STATE, (2 * g + 1) * STATE)
         r_at = slice((2 * g + 1) * STATE, (2 * g + 2) * STATE)
-        inc = excl[0, :, cols].astype(bf16)
-        outg = excl[1, :, cols].astype(bf16)
+        inc = excl[0, :, cols]
+        outg = excl[1, :, cols]
         dval[:, cols] = (acc_g[:, cols] + end_x[:, cols] * nn(pairs[:, w_at], outg)).astype(bf16)
         ds = dscore[g].astype(bf16)
         dpair[:, w_at] = (tn(ds, pairs[:, r_at]) + nt(tv[:, cols], outg)).astype(bf16)
@@ -414,12 +410,8 @@
 
     for c in [x_own, g_own] + x_far + x_fwd + g_far + g_fwd:
         c.wait_send()
-    for way in (0, 1):
-        for k in range(steps):
-            @pl.when(can_send(way, k))
-            def _():
-                for c in copies[way * steps + k]:
-                    c.wait_send()
+    for c in d_copies + there[0] + there[1] + back[0] + back[1]:
+        c.wait_send()
 
 
 def per_device(
@@ -431,7 +423,9 @@
     pwid = state_weight.shape[1]
     heads = log_decay.shape[0]
     groups = pwid // (2 * STATE)
-    steps = max(n_seq - 1, 0).bit_length()
+    row_cuts = min(n_seq, STATE // 16)
+    piece = (n_seq, STATE // row_cuts, vwid // (n_seq // row_cuts))
+    sems = 32 * n_head + 5 * n_seq
     chips = n_head // 2
     per = max(chips - 1, 1)
     vm = pltpu.VMEM
@@ -445,16 +439,16 @@
         vm((heads, 1, rows), f32), vm((heads, 1, rows), f32),
         vm((groups, rows, rows), f32), vm((groups, rows, rows), f32),
         vm((rows, vwid), bf16), vm((rows, vwid), bf16),
-        vm((2, STATE, vwid), f32), vm((2, STATE, vwid), f32),
-        vm((2, 8, vwid), f32), vm((2, 8, vwid), f32),
-        vm((2, steps, STATE, vwid), bf16), vm((2, steps, STATE, vwid), bf16),
-        vm((2, steps, 8, vwid), f32), vm((2, steps, 8, vwid), f32),
+        vm((2, STATE, vwid), f32), vm((2, STATE, vwid), bf16),
+        vm((2,) + piece, bf16), vm((2,) + piece, bf16),
+        vm((2,) + piece, bf16), vm((2,) + piece, bf16),
+        vm((8, 128), f32), vm((n_seq, 8, 128), f32), vm((n_seq, 8, vwid), f32),
         vm((2, per, rows, width), bf16), vm((2, per, rows, width), bf16),
         vm((2, per, rows, width), bf16), vm((2, per, rows, width), bf16),
         vm((2, rows, width), bf16), vm((2, rows, width), bf16),
         vm((2, rows, width), f32),
-        pltpu.SemaphoreType.DMA((SEMS,)),
-        pltpu.SemaphoreType.DMA((SEMS,)),
+        pltpu.SemaphoreType.DMA((sems,)),
+        pltpu.SemaphoreType.DMA((sems,)),
         pltpu.SemaphoreType.DMA((3 * n_head,)),
     ]
     vspec = pl.BlockSpec(memory_space=vm)

time: 92.4 us -> 78.9 us (0.85)
  the two profiles are of different devices: /device:TPU:11 before, /device:TPU:0 now
where the time goes in v2:
time: 78.9 us; the launch traced here: 78.7 us
  Pallas kernels  74.3 us (94%)
  local copies, waits for them, and re-layouts  3.74 us (5%)
    pallas_call x1, Pallas kernels, per_device(): pl.pallas_call(functools.partial(kernel, n_head, n_seq), out_shape=(jax.S...  74.3 us
    unnamed x2, local copies, waits for them, and re-layouts  3.74 us

profile of v2, /device:TPU:0, one launch (start us, length us, event | category | flops | bytes accessed | tf_op | source)
XLA Modules:
  0.0 78.7 jit_solution(13545205412232800355)
XLA Ops:
  0.6 74.3 %shard_map.86 = (bf16[256,1024]{1,0:T(8,128)(2,1)}, bf16[256,1024]{1,0:T(8,128)(2,1)}) custom-call(bf16[256,1024]{1,0:T(8,128)(2,1)} %x_ref.1, bf16[256,1024]{1,0:T(8,128)(2,1)} %g_ref.1, f32[16,256]{1,0:T(8,128)} %ld_ref.1, f32[16]{0:T(128)} %skip_ref.1, bf16[4096,1024]{1,0:T(8,128)(2,1)} %vw_hbm.1, bf16[4096,512]{1,0:T(8,128)(2,1)} %sw_hbm.1, ...), custom_call_target="tpu_custom_call" | custom-call | flops 10737418240 | bytes 20971520 | tf_op jit(solution)/shard_map/pallas_call | solution.py:457
  74.9 1.9 %copy.11 = bf16[256,1024]{1,0:T(8,128)(2,1)} copy(bf16[256,1024]{1,0:T(8,128)(2,1)} %get-tuple-element.4) | data formatting | bytes 1048576
  76.8 1.9 %copy.12 = bf16[256,1024]{1,0:T(8,128)(2,1)} copy(bf16[256,1024]{1,0:T(8,128)(2,1)} %get-tuple-element.5) | data formatting | bytes 1048576

commit v3 on v2

--- a/solution.py
+++ b/solution.py
@@ -45,7 +45,7 @@
     ent_x, end_x, run_x, run_r, inf_r, score, dscore, tv, eg,
     total, excl, sendb, recvb, backb, backr, sendd, recvd, dec,
     p_send, p_recv, y_send, y_recv, o_send, o_recv, part,
-    ssem, rsem, wsem,
+    weight, mask, ssem, rsem, wsem,
 ):
     rows, width = x_ref.shape
     vwid = vw.shape[1]
@@ -98,12 +98,15 @@
             three.append(pltpu.make_async_copy(a, b, wsem.at[wcount]))
             wcount += 1
         wcopies.append(three)
+    x_here = pltpu.make_async_copy(x_ref, xs.at[hi], wsem.at[wcount])
+    g_here = pltpu.make_async_copy(g_ref, gs.at[hi], wsem.at[wcount + 1])
+    for peer in peers:
+        pl.semaphore_signal(barrier, inc=1, device_id=peer, device_id_type=MESH)
+    x_here.start()
     for three in wcopies:
         three[0].start()
         three[1].start()
-
-    for peer in peers:
-        pl.semaphore_signal(barrier, inc=1, device_id=peer, device_id_type=MESH)
+    g_here.start()
     pl.semaphore_wait(barrier, len(peers))
 
     crow = rows // CHUNKS
@@ -179,7 +182,8 @@
 
     wcopies[0][0].wait()
     wcopies[0][1].wait()
-    mul_x(hi, x_ref, True)
+    x_here.wait()
+    mul_x(hi, xs.at[hi], True)
     x_own.wait_recv()
     wcopies[1][0].wait()
     wcopies[1][1].wait()
@@ -190,8 +194,6 @@
             x_far[k * per + j].wait_recv()
             x_fwd[k * per + j].start()
             g_far[k * per + j].start()
-    wcopies[0][2].wait()
-    mul_g(hi, g_ref, True)
     for j in range(per):
         src = at_chip(chips - 1 - j, core)
         for which in (0, 1):
@@ -260,6 +262,33 @@
         r_at = slice((2 * g + 1) * STATE, (2 * g + 2) * STATE)
         score[g] = nt(pairs[:, r_at], pairs[:, w_at])
         dscore[g] = jnp.zeros((rows, rows), f32)
+
+    wcopies[0][2].wait()
+    g_here.wait()
+    mul_g(hi, gs.at[hi], True)
+    per_group = gwid // pair
+
+    @pl.loop(0, heads // 2)
+    def _(i):
+        g = i // per_group
+        at = pl.ds(pl.multiple_of(i * pair, pair), pair)
+        left = lax.broadcasted_iota(jnp.int32, (rows, pair), 1) < hdim
+        causal = lax.broadcasted_iota(jnp.int32, (rows, rows), 0) >= lax.broadcasted_iota(
+            jnp.int32, (rows, rows), 1
+        )
+        vp = values[:, at]
+        rx = run_x[:, at]
+        s = score[g]
+        gain = jnp.where(left, skip_ref[2 * i], skip_ref[2 * i + 1])
+        outs = []
+        for h in (0, 1):
+            rc = rx[:, h * hdim : h * hdim + 1]
+            m = jnp.exp(jnp.where(causal, rc - run_r[2 * i + h], -1e30)) * inf_r[2 * i + h]
+            w = (s * m).astype(bf16)
+            mask[2 * i + h] = m.astype(bf16)
+            weight[2 * i + h] = w
+            outs.append(nn(w, vp))
+        acc_v[:, at] = jnp.where(left, outs[0], outs[1]) + gain * vp.astype(f32)
 
     g_own.wait_recv()
     wcopies[1][2].wait()
@@ -286,95 +315,90 @@
         total[1, :, cols] = tn(pairs[:, r_at], eg[:, cols])
     scan_begin(1)
 
-    per_group = gwid // pair
-
-    def within(begin, end):
-        @pl.loop(begin, end)
+    def within_back():
+        @pl.loop(0, heads // 2)
         def _(i):
             g = i // per_group
             at = pl.ds(pl.multiple_of(i * pair, pair), pair)
             left = lax.broadcasted_iota(jnp.int32, (rows, pair), 1) < hdim
-            causal = lax.broadcasted_iota(jnp.int32, (rows, rows), 0) >= lax.broadcasted_iota(
-                jnp.int32, (rows, rows), 1
-            )
             vp = values[:, at]
             gp = mgrad[:, at]
             gp32 = gp.astype(f32)
-            rx = run_x[:, at]
-            s = score[g]
             gain = jnp.where(left, skip_ref[2 * i], skip_ref[2 * i + 1])
-            outs, grads, ds = [], [], None
+            grads, ds = [], None
             for h in (0, 1):
-                rc = rx[:, h * hdim : h * hdim + 1]
-                m = jnp.exp(jnp.where(causal, rc - run_r[2 * i + h], -1e30)) * inf_r[2 * i + h]
-                w = (s * m).astype(bf16)
-                outs.append(nn(w, vp))
-                grads.append(tn(w, gp))
+                grads.append(tn(weight[2 * i + h], gp))
                 gh = jnp.where(left == (h == 0), gp32, 0.0).astype(bf16)
-                d = m * nt(gh, vp)
+                d = mask[2 * i + h].astype(f32) * nt(gh, vp)
                 ds = d if ds is None else ds + d
-            acc_v[:, at] = jnp.where(left, outs[0], outs[1]) + gain * vp.astype(f32)
             acc_g[:, at] = jnp.where(left, grads[0], grads[1]) + gain * gp32
             dscore[g] = dscore[g] + ds
 
-    within(0, heads // 2)
     scan_end(0)
 
-    def tiles(partial, dest, use):
-        @pl.loop(0, width // TILE)
+    half = width // 2
+    parts = (0, 1)
+
+    def tiles(partial, dest, c, use):
+        @pl.loop(0, half // TILE)
         def _(n):
-            use(pl.ds(pl.multiple_of(n * TILE, TILE), TILE), partial(dest * width + n * TILE))
-
-    def scatter_copies(u):
+            at = pl.ds(pl.multiple_of(n * TILE, TILE), TILE)
+            use(at, partial(dest * width + c * half + n * TILE))
+
+    def scatter_begin(u, partial):
         near = [
-            remote(p_send.at[u, j], p_recv.at[u, j], {"head": partner}) for j in range(per)
+            [remote(p_send.at[u, j, c], p_recv.at[u, j, c], {"head": partner}) for c in parts]
+            for j in range(per)
         ]
         far = [
-            remote(y_send.at[u, j], y_recv.at[u, j], {"head": at_chip(j + 1, core)})
+            [
+                remote(y_send.at[u, j, c], y_recv.at[u, j, c], {"head": at_chip(j + 1, core)})
+                for c in parts
+            ]
             for j in range(per)
         ]
-        own = remote(o_send.at[u], o_recv.at[u], {"head": partner})
-        return near, far, own
-
-    def scatter_begin(u, partial):
-        near, far, own = scatter_copies(u)
+        own = [remote(o_send.at[u, c], o_recv.at[u, c], {"head": partner}) for c in parts]
         for j in range(per):
-            def keep(at, p):
-                p_send[u, j, :, at] = p.astype(bf16)
-
-            tiles(partial, at_chip(j + 1, 1 - core), keep)
-            near[j].start()
+            for c in parts:
+                def keep(at, p):
+                    p_send[u, j, c, :, at] = p.astype(bf16)
+
+                tiles(partial, at_chip(j + 1, 1 - core), c, keep)
+                near[j][c].start()
         for j in range(per):
-            def keep_part(at, p):
-                part[u, :, at] = p
-
-            tiles(partial, at_chip(j + 1, core), keep_part)
-            near[j].wait_recv()
-            y_send[u, j] = (part[u] + p_recv[u, j].astype(f32)).astype(bf16)
-            far[j].start()
-
-        def keep_own(at, p):
-            o_send[u, :, at] = p.astype(bf16)
-
-        tiles(partial, partner, keep_own)
-        own.start()
-
-        def keep_mine(at, p):
-            part[u, :, at] = p
-
-        tiles(partial, hi, keep_mine)
+            for c in parts:
+                def keep_part(at, p):
+                    part[u, c, :, at] = p
+
+                tiles(partial, at_chip(j + 1, core), c, keep_part)
+                near[j][c].wait_recv()
+                y_send[u, j, c] = (part[u, c] + p_recv[u, j, c].astype(f32)).astype(bf16)
+                far[j][c].start()
+        for c in parts:
+            def keep_own(at, p):
+                o_send[u, c, :, at] = p.astype(bf16)
+
+            tiles(partial, partner, c, keep_own)
+            own[c].start()
+        for c in parts:
+            def keep_mine(at, p):
+                part[u, c, :, at] = p
+
+            tiles(partial, hi, c, keep_mine)
         return near, far, own
 
     def scatter_end(u, three, o_ref):
         near, far, own = three
-        own.wait_recv()
-        s = part[u] + o_recv[u].astype(f32)
-        for j in range(per):
-            far[j].wait_recv()
-            s = s + y_recv[u, j].astype(f32)
-        o_ref[...] = s.astype(bf16)
-        for c in near + far + [own]:
-            c.wait_send()
+        for c in parts:
+            own[c].wait_recv()
+            s = part[u, c] + o_recv[u, c].astype(f32)
+            for j in range(per):
+                far[j][c].wait_recv()
+                s = s + y_recv[u, j, c].astype(f32)
+            o_ref[:, c * half : (c + 1) * half] = s.astype(bf16)
+        for c in parts:
+            for copy in [n[c] for n in near] + [f[c] for f in far] + [own[c]]:
+                copy.wait_send()
 
     for g in range(groups):
         cols = slice(g * gwid, (g + 1) * gwid)
@@ -387,6 +411,7 @@
 
     first_rs = scatter_begin(0, out_partial)
 
+    within_back()
     scan_mid(1)
     scan_end(1)
     for g in range(groups):
@@ -412,6 +437,15 @@
         c.wait_send()
     for c in d_copies + there[0] + there[1] + back[0] + back[1]:
         c.wait_send()
+
+
+def place(a_ref, b_ref, a_out, b_out, sem):
+    first = pltpu.make_async_copy(a_ref, a_out, sem.at[0])
+    second = pltpu.make_async_copy(b_ref, b_out, sem.at[1])
+    first.start()
+    second.start()
+    first.wait()
+    second.wait()
 
 
 def per_device(
@@ -443,24 +477,25 @@
         vm((2,) + piece, bf16), vm((2,) + piece, bf16),
         vm((2,) + piece, bf16), vm((2,) + piece, bf16),
         vm((8, 128), f32), vm((n_seq, 8, 128), f32), vm((n_seq, 8, vwid), f32),
-        vm((2, per, rows, width), bf16), vm((2, per, rows, width), bf16),
-        vm((2, per, rows, width), bf16), vm((2, per, rows, width), bf16),
-        vm((2, rows, width), bf16), vm((2, rows, width), bf16),
-        vm((2, rows, width), f32),
+        vm((2, per, 2, rows, width // 2), bf16), vm((2, per, 2, rows, width // 2), bf16),
+        vm((2, per, 2, rows, width // 2), bf16), vm((2, per, 2, rows, width // 2), bf16),
+        vm((2, 2, rows, width // 2), bf16), vm((2, 2, rows, width // 2), bf16),
+        vm((2, 2, rows, width // 2), f32),
+        vm((heads, rows, rows), bf16), vm((heads, rows, rows), bf16),
         pltpu.SemaphoreType.DMA((sems,)),
         pltpu.SemaphoreType.DMA((sems,)),
-        pltpu.SemaphoreType.DMA((3 * n_head,)),
+        pltpu.SemaphoreType.DMA((3 * n_head + 2,)),
     ]
     vspec = pl.BlockSpec(memory_space=vm)
     anys = pl.BlockSpec(memory_space=pl.ANY)
     flops = 2 * rows * full * (3 * vwid + pwid) + 2 * rows * full * (vwid + pwid)
-    return pl.pallas_call(
+    made = pl.pallas_call(
         functools.partial(kernel, n_head, n_seq),
         out_shape=(
             jax.ShapeDtypeStruct((rows, width), bf16),
             jax.ShapeDtypeStruct((rows, width), bf16),
         ),
-        in_specs=[vspec, vspec, vspec, pl.BlockSpec(memory_space=pltpu.SMEM), anys, anys, anys],
+        in_specs=[anys, anys, vspec, pl.BlockSpec(memory_space=pltpu.SMEM), anys, anys, anys],
         out_specs=(vspec, vspec),
         scratch_shapes=scratch,
         compiler_params=pltpu.CompilerParams(
@@ -470,6 +505,13 @@
             flops=flops, bytes_accessed=2 * full * (2 * vwid + pwid), transcendentals=0
         ),
     )(layer_input, output_grad, log_decay, skip_gain, value_weight, state_weight, output_weight)
+    return pl.pallas_call(
+        place,
+        out_shape=tuple(jax.ShapeDtypeStruct(a.shape, a.dtype) for a in made),
+        in_specs=[anys, anys],
+        out_specs=(anys, anys),
+        scratch_shapes=[pltpu.SemaphoreType.DMA((2,))],
+    )(*made)
 
 
 def solution(mesh):

time: 78.9 us -> 110 us (1.39)
  Pallas kernels: 74.3 us -> 109 us
  local copies, waits for them, and re-layouts: 3.74 us -> 0 us
    pallas_call x0 -> x1, Pallas kernels: none -> 32.9 us  [per_device(): pl.pallas_call(place, out_shape=tuple((jax.ShapeDtypeStruct(a.shape, a.dt...]
    unnamed x2 -> x0, local copies, waits for them, and re-layouts: 3.74 us -> none
    pallas_call x1, Pallas kernels: 74.3 us -> 76.2 us  [per_device(): pl.pallas_call(functools.partial(kernel, n_head, n_seq), out_shape=(jax.S...]
where the time goes in v3:
time: 110 us
  Pallas kernels  109 us (99%)
    pallas_call x1, Pallas kernels, per_device(): pl.pallas_call(functools.partial(kernel, n_head, n_seq), out_shape=(jax.S...  76.2 us
    pallas_call x1, Pallas kernels, per_device(): pl.pallas_call(place, out_shape=tuple((jax.ShapeDtypeStruct(a.shape, a.dt...  32.9 us

profile of v3, /device:TPU:0, one launch (start us, length us, event | category | flops | bytes accessed | tf_op | source)
XLA Modules:
  0.0 109.8 jit_solution(9969542882119499357)
XLA Ops:
  0.6 76.2 %shard_map.86 = (bf16[256,1024]{1,0:T(8,128)(2,1)}, bf16[256,1024]{1,0:T(8,128)(2,1)}) custom-call(bf16[256,1024]{1,0:T(8,128)(2,1)} %x_ref.1, bf16[256,1024]{1,0:T(8,128)(2,1)} %g_ref.1, f32[16,256]{1,0:T(8,128)} %ld_ref.1, f32[16]{0:T(128)} %skip_ref.1, bf16[4096,1024]{1,0:T(8,128)(2,1)} %vw_hbm.1, bf16[4096,512]{1,0:T(8,128)(2,1)} %sw_hbm.1, ...), custom_call_target="tpu_custom_call" | custom-call | flops 10737418240 | bytes 20971520 | tf_op jit(solution)/shard_map/pallas_call | solution.py:492
  76.8 32.9 %shard_map.87 = (bf16[256,1024]{1,0:T(8,128)(2,1)}, bf16[256,1024]{1,0:T(8,128)(2,1)}) custom-call(bf16[256,1024]{1,0:T(8,128)(2,1)} %get-tuple-element.4.a_ref, bf16[256,1024]{1,0:T(8,128)(2,1)} %get-tuple-element.5.b_ref), custom_call_target="tpu_custom_call" | custom-call | tf_op jit(solution)/shard_map/pallas_call | solution.py:508
